TPU v7x, 512 devices: a whole 4x8x8 slice. The times are simulated.
512 devices in a mesh: src: 32 (over z, x), dst: 16 (over y, core).
Axes of the slice: x: 4, y: 8, z: 8, core: 2. Of those that a mesh axis runs over, the one named last changes fastest.
Arguments:
- src_table: bfloat16 [16384, 400], P(('src', 'dst')), may hold values from -2.5 to 2.5
- dst_table: bfloat16 [12288, 400], P(('dst', 'src')), may hold values from -2.5 to 2.5
- rel_diag: float32 [512, 400], replicated, may hold values from 0.1 to 1.9
- src_index: int32 [32, 16, 512], P('src', 'dst'), may hold values from 0 to 511
- dst_index: int32 [32, 16, 512], P('src', 'dst'), may hold values from 0 to 767
- rel_index: int32 [32, 16, 512], P('src', 'dst'), may hold values from 0 to 511
- neg_index: int32 [32, 16, 2, 512], P('src', 'dst'), may hold values from 0 to 767
- edge_count: int32 [32, 16], P('src', 'dst'), may hold values from 32 to 512, as said below
Outputs:
- grad_src: float32 [16384, 400], P(('src', 'dst'))
- grad_dst: float32 [12288, 400], P(('dst', 'src'))
- grad_rel: float32 [512, 400], replicated
Inputs may be any that keep to these rules, and one draw needn't show every extreme that they name: Edge slots 0 to edge_count[a, b] - 1 of bucket (a, b) are live and the rest are ignored; some bucket has exactly 512 live edges and some has exactly 32.
All inputs are finite; a program needn't handle non-finite values.
Results may differ from a plain program's by a relative error of at most 0.0021.
Values may be sent and summed in bfloat16 or wider, within the bound.
A program may use at most 64 MiB of HBM per device.

v0:
```python
import math

import jax
import jax.numpy as jnp
from jax import lax
from jax.sharding import PartitionSpec as P


def per_device(
    src_table, dst_table, rel_diag, src_index, dst_index, rel_index, neg_index, edge_count
):
    source_part = lax.all_gather(src_table, "dst", axis=0, tiled=True)
    target_part = lax.all_gather(dst_table, "src", axis=0, tiled=True)
    source_rows = src_index[0, 0]
    target_rows = dst_index[0, 0]
    relation_rows = rel_index[0, 0]
    negative_rows = neg_index[0, 0]
    live_count = edge_count[0, 0]
    spans, negs = negative_rows.shape
    edges = source_rows.shape[0]
    width = src_table.shape[1]
    per_span = edges // spans
    inverse = 1.0 / math.sqrt(negs)
    live_mask = (jnp.arange(edges, dtype=jnp.int32) < live_count).astype(jnp.float32)
    source_vec = jnp.take(source_part, source_rows, axis=0).astype(jnp.float32)
    target_vec = jnp.take(target_part, target_rows, axis=0).astype(jnp.float32)
    relation_vec = jnp.take(rel_diag, relation_rows, axis=0)
    scaled = source_vec * relation_vec
    rounded = scaled.astype(jnp.bfloat16)
    positive = jnp.sum(scaled * target_vec, axis=1)
    weight_pos = -live_mask * jax.nn.sigmoid(-positive)
    negative_vec = jnp.take(target_part, negative_rows.reshape(-1), axis=0).reshape(
        spans, negs, width
    )
    grouped = rounded.reshape(spans, per_span, width)
    scores = jnp.einsum("ced,cnd->cen", grouped, negative_vec, preferred_element_type=jnp.float32)
    weight_neg = (live_mask.reshape(spans, per_span, 1) * jax.nn.sigmoid(scores) * inverse).astype(
        jnp.bfloat16
    )
    pulled = jnp.einsum(
        "cen,cnd->ced", weight_neg, negative_vec, preferred_element_type=jnp.float32
    ).reshape(edges, width)
    pushed = jnp.einsum("cen,ced->cnd", weight_neg, grouped, preferred_element_type=jnp.float32)
    grad_mix = weight_pos[:, None] * target_vec + pulled
    source_grad = (
        jnp.zeros((source_part.shape[0], width), jnp.float32)
        .at[source_rows]
        .add(relation_vec * grad_mix)
    )
    relation_grad = (
        jnp.zeros(rel_diag.shape, jnp.float32).at[relation_rows].add(source_vec * grad_mix)
    )
    pos_push = weight_pos[:, None] * scaled
    flat_push = pushed.reshape(spans * negs, width)
    flat_rows = negative_rows.reshape(-1)
    source_out = lax.psum_scatter(source_grad, "dst", scatter_dimension=0, tiled=True)
    target_grad = (
        jnp.zeros((target_part.shape[0], width), jnp.float32).at[target_rows].add(pos_push)
    )
    target_grad = target_grad.at[flat_rows].add(flat_push)
    target_out = lax.psum_scatter(target_grad, "src", scatter_dimension=0, tiled=True)
    relation_out = lax.psum(relation_grad, ("src", "dst"))
    return (source_out, target_out, relation_out)


def solution(mesh):
    return jax.shard_map(
        per_device,
        mesh=mesh,
        in_specs=(
            P(("src", "dst"), None),
            P(("dst", "src"), None),
            P(),
            P("src", "dst", None),
            P("src", "dst", None),
            P("src", "dst", None),
            P("src", "dst", None, None),
            P("src", "dst"),
        ),
        out_specs=(P(("src", "dst"), None), P(("dst", "src"), None), P()),
        check_vma=False,
    )
```

profile of v0, /device:TPU:1, one launch (start us, length us, event | category | flops | bytes accessed | tf_op | source)
XLA Modules:
  0.0 407.2 jit_solution(11791868908301941031)
XLA Ops:
  8.0 0.7 compare_select_fusion.4
  9.2 1.3 reduce.7
  10.6 1.3 reduce.6
  11.9 0.7 compare_select_fusion.3
  12.6 1.3 compare_and_fusion
  13.9 0.7 copy.29
  15.2 1.3 compare_and_fusion.5
  16.5 0.7 compare_select_fusion.2
  17.2 0.6 squeeze.29
  17.8 0.6 squeeze.30
  18.4 0.6 compare_convert_fusion
  18.9 0.6 pad_clamp_fusion.2
  20.1 22.7 %all_gather.6 = bf16[512,400]{1,0:T(8,128)(2,1)S(1)} all-gather(bf16[32,400]{1,0:T(8,128)(2,1)} %param.8), channel_id=1, replica_groups=mesh['src'=32,'dst'=16] {'dst'}, dimensions={0}, use_global_device_ids=true | all-gather | bytes 435200 | tf_op jit(solution)/shard_map/all_gather | solution.py:12
  42.8 2.0 gather_fusion.1
  45.0 42.3 %all_gather.7 = bf16[768,400]{1,0:T(8,128)(2,1)S(1)} all-gather(bf16[24,400]{1,0:T(8,128)(2,1)S(1)} %copy-done.7), channel_id=1, replica_groups=mesh['src'=32,'dst'=16] {'src'}, dimensions={0}, use_global_device_ids=true | all-gather | bytes 633600 | tf_op jit(solution)/shard_map/all_gather | solution.py:13
  87.3 2.0 gather_fusion.2
  89.2 4.0 gather_fusion.3
  93.2 1.2 copy.19
  94.4 1.5 copy.16
  95.9 1.8 gather_fusion
  98.5 1.0 copy-done.3
  99.5 0.6 fusion.5
  101.5 0.6 copy-done.8
  102.3 4.9 %scatter_custom_fusion.3 = f32[512,400]{1,0:T(8,128)} fusion(s32[512]{0:T(512)} %bitcast.46, f32[512,400]{1,0:T(8,128)S(1)} %fusion.8, f32[]{:T(128)} %constant.37.clone.1, bf16[512,400]{1,0:T(8,128)(2,1)S(1)} %gather_fusion.1, pred[512]{0:T(512)(128)(4,1)S(1)} %get-tuple-element.12), kind=kCustom, calls=%fused_computation.19 | custom fusion | flops 819200 | bytes 2049024 | tf_op jit(solution)/shard_map/scatter-add | solution.py:51
  107.5 4.8 %scatter_custom_fusion = f32[512,400]{1,0:T(8,128)} fusion(s32[512]{0:T(512)} %bitcast.44, f32[512,400]{1,0:T(8,128)S(1)} %fusion.8, f32[512,400]{1,0:T(8,128)S(1)} %gather_fusion, f32[]{:T(128)} %constant.47.clone.1, f32[]{:T(128)} %constant.37.clone.1, pred[512]{0:T(512)(128)(4,1)S(1)} %copy-done.10), kind=kCustom, calls=%fused_computation.24 | custom fusion | flops 614400 | bytes 2459136 | tf_op jit(solution)/shard_map/scatter-add | solution.py:48
  112.4 4.5 %scatter_custom_fusion.1 = f32[768,400]{1,0:T(8,128)S(1)} fusion(s32[512]{0:T(512)} %bitcast.42, f32[]{:T(128)} %constant.37.clone.1, f32[512,400]{1,0:T(8,128)S(1)} %gather_fusion, f32[512]{0:T(512)} %copy-done.8, f32[]{:T(128)} %constant.47.clone.1, pred[512]{0:T(512)(128)(4,1)} %compare_and_fusion.5, bf16[512,400]{1,0:T(8,128)(2,1)S(1)} %gather_fusion.1, ...), kind=kCustom, calls=%fused_computation.22 | custom fusion | flops 1228800 | bytes 2461696 | tf_op jit(solution)/shard_map/scatter-add | solution.py:58
  117.0 2.9 fusion.27
  119.8 7.8 %scatter_fusion = f32[768,400]{1,0:T(8,128)S(1)} fusion(f32[768,400]{1,0:T(8,128)S(1)} %scatter_custom_fusion.1, s32[1024]{0:T(1024)S(1)} %bitcast.37, f32[1024,400]{1,0:T(8,128)} %bitcast.34), kind=kCustom, calls=%fused_computation.6 | custom fusion | flops 409600 | bytes 4919296 | tf_op jit(solution)/shard_map/scatter-add | solution.py:60
  127.7 1.1 copy-done
  128.9 258.4 %all-reduce.2.cloned.1.call-done = f32[512,400]{1,0:T(8,128)} async-done(((f32[512,400]{1,0:T(8,128)}), f32[512,400]{1,0:T(8,128)}) %all-reduce.2.cloned.1.call-update) | async-done | bytes 819216 | tf_op jit(solution)/shard_map/psum | solution.py:62
  387.2 2.4 copy.24
  389.7 10.1 %reduce-scatter.5.cloned.1.call-done = f32[24,400]{1,0:T(8,128)} async-done(((f32[768,400]{1,0:T(8,128)}), f32[24,400]{1,0:T(8,128)}) %reduce-scatter.5.cloned.1.call-update) | async-done | bytes 38416 | tf_op jit(solution)/shard_map/reduce_scatter | solution.py:61
  (58 shorter events, 4.1 us)
Async XLA Ops:
  8.0 379.2 %all-reduce.2.cloned.1.call-start = ((), (), s32[]{:S(2)}) async-start(), calls=%async_computation.4 | async-start | bytes 2097152 | tf_op jit(solution)/shard_map/psum | solution.py:62
  8.7 10.9 %copy-start.13 = (s32[512,1]{0,1:T(1,128)}, s32[512,1]{0,1:T(1,128)S(1)}, u32[]{:S(2)}) copy-start(s32[512,1]{0,1:T(1,128)S(1)} %compare_select_fusion.4) | copy-start | bytes 6148
  12.6 7.0 %copy-start.14 = (s32[512,1]{0,1:T(1,128)}, s32[512,1]{0,1:T(1,128)S(1)}, u32[]{:S(2)}) copy-start(s32[512,1]{0,1:T(1,128)S(1)} %compare_select_fusion.3) | copy-start | bytes 6148
  17.2 2.4 copy-start.12
  19.6 0.6 copy-start.5
  42.8 2.2 copy-start.7
  97.7 0.7 copy-start.15
  97.7 0.7 copy-start.16
  97.7 0.8 copy-start.18
  97.7 0.8 copy-start.19
  98.4 1.1 copy-start.3
  99.5 0.8 copy-start.1
  100.3 1.2 copy-start.4
  100.3 0.7 copy-start.9
  100.3 0.7 copy-start.17
  100.3 0.8 copy-start.10
  101.0 1.3 copy-start.11
  101.5 0.6 copy-start.8
  107.3 282.4 %reduce-scatter.3.cloned.1.call-start = ((), (), s32[]{:S(2)}) async-start(), calls=%async_computation.2 | async-start | bytes 1114112 | tf_op jit(solution)/shard_map/reduce_scatter | solution.py:56
  112.4 4.6 %copy-start.2 = (bf16[2,256,400]{1,2,0:T(8,128)(2,1)S(1)}, bf16[2,256,400]{1,2,0:T(8,128)(2,1)}, u32[]{:S(2)}) copy-start(bf16[2,256,400]{1,2,0:T(8,128)(2,1)} %copy-done.1) | copy-start | bytes 1228804
  112.4 287.4 %reduce-scatter.5.cloned.1.call-start = ((), (), s32[]{:S(2)}) async-start(), calls=%async_computation.3 | async-start | bytes 1622016 | tf_op jit(solution)/shard_map/reduce_scatter | solution.py:61
  116.9 2.9 copy-start.6
  127.7 1.2 copy-start
Sparse Core Ops, SparseCore 0:
  107.4 279.7 all-reduce.1
Sparse Core Ops, SparseCore 1:
  112.5 64.2 reduce-scatter.2
  182.2 217.5 reduce-scatter.4
where the time goes:
time: 412 us; the launch traced here: 407 us
  waiting for transfers between devices  268 us (65%)
  blocking collectives  64.9 us (16%)
  other arithmetic  31.4 us (8%)
  local copies, waits for them, and re-layouts  21.7 us (5%)
  between operations  16.4 us (4%)
    psum x1, waiting for transfers between devices, per_device(): relation_out = lax.psum(relation_grad, ('src', 'dst'))  258 us
    all_gather x1, blocking collectives, per_device(): target_part = lax.all_gather(dst_table, 'src', axis=0, tiled=True)  42.3 us
    all_gather x1, blocking collectives, per_device(): source_part = lax.all_gather(src_table, 'dst', axis=0, tiled=True)  22.7 us
    reduce_scatter x1, waiting for transfers between devices, per_device(): lax.psum_scatter(target_grad, 'src', scatter_dimension=0, tiled=True)  10.1 us
    unnamed x44, local copies, waits for them, and re-layouts  9.16 us
  transfers between devices with their start and end apart: 3, of which 2 were waited for; matrix products, arithmetic and copies ran while one was open for 6% of the time, Pallas kernels for 0%

commit v1 on v0

v1 whole, which is shorter than its diff:
```python
import functools
import math

import jax
import jax.numpy as jnp
from jax import lax
from jax.experimental import pallas as pl
from jax.experimental.pallas import tpu as pltpu
from jax.sharding import PartitionSpec as P

F32, BF16, I32 = jnp.float32, jnp.bfloat16, jnp.int32
NX, NC = 4, 2
SEMS = 160


def dot(a, b):
    return jnp.dot(a, b, preferred_element_type=F32)


def dot_nt(a, b):
    return lax.dot_general(a, b, (((1,), (1,)), ((), ())), preferred_element_type=F32)


def split2(v):
    hi = v.astype(BF16)
    return hi, (v - hi.astype(F32)).astype(BF16)


def kernel(
    nz, nx, ny,
    src_ref, dst_ref, rel_ref, si_ref, di_ref, ri_ref, ni_ref, cnt_ref,
    out_s, out_d, out_r,
    S, T, RF, hot_s, hot_d, hot_r, cold_s, cold_d, cold_r, counts, r_v, q_v, g_v, s_v, t_v, w_v, qb_v, uh_v, ul_v,
    rel_part, rel_sib, rel_xs, rel_xr, rel_zs, rel_zr, rel_ys, rel_yr,
    dst_xs, dst_part, dst_xr, dst_zs, dst_zr,
    src_part, src_sib, src_ys, src_yr,
    send, recv,
):
    a, b = lax.axis_index("src"), lax.axis_index("dst")
    z, x = a // nx, lax.rem(a, nx)
    y, c = b // NC, lax.rem(b, NC)
    o = 1 - c
    rows_s, width = src_ref.shape
    rows_d = dst_ref.shape[0]
    half_s = ny * rows_s
    part_d = nz * rows_d
    n_dst = nx * part_d
    n_rel = rel_ref.shape[0]
    half_r = n_rel // NC
    quart_r = half_r // nx
    edges = si_ref.shape[-1]
    spans, negs = ni_ref.shape[-2], ni_ref.shape[-1]
    per = edges // spans
    inverse = 1.0 / math.sqrt(negs)

    def at_z(k):
        return lax.rem(z + k, nz)

    def at_x(k):
        return lax.rem(x + k, nx)

    def at_y(k):
        return lax.rem(y + k, ny)

    def dev(zz=z, xx=x, yy=y, cc=c):
        return (zz * nx + xx, yy * NC + cc)

    slots = {}
    live_copies = []

    def slot(key):
        return slots.setdefault(key, len(slots))

    def copy(key, src, dst, target):
        k = slot(key)
        return pltpu.make_async_remote_copy(
            src_ref=src, dst_ref=dst, send_sem=send.at[k], recv_sem=recv.at[k],
            device_id=target, device_id_type=pl.DeviceIdType.MESH,
        )

    def start(key, src, dst, target):
        d = copy(key, src, dst, target)
        d.start()
        live_copies.append(d)

    def arrived(key, dst):
        copy(key, dst, dst, dev(cc=o)).wait_recv()

    barrier = pltpu.get_barrier_semaphore()
    peers = [dev(cc=o)]
    peers += [dev(zz=at_z(k)) for k in range(1, nz)]
    peers += [dev(yy=at_y(k)) for k in range(1, ny)]
    peers += [dev(xx=at_x(k)) for k in range(1, nx)]
    for p in peers:
        pl.semaphore_signal(barrier, inc=1, device_id=p, device_id_type=pl.DeviceIdType.MESH)
    S[c, y] = src_ref[...]
    T[x, z] = dst_ref[...]
    pl.semaphore_wait(barrier, len(peers))

    for k in range(1, nz):
        start(("tz", k), dst_ref, T.at[x, z], dev(zz=at_z(k)))
    for k in range(1, ny):
        start(("sy", k), src_ref, S.at[c, y], dev(yy=at_y(k)))
    for e in range(1, nx):
        start(("tx", e, 0), dst_ref, T.at[x, z], dev(xx=at_x(e)))
    start(("sc", 0), src_ref, S.at[c, y], dev(cc=o))

    lx, ls = nx.bit_length() - 1, rows_s.bit_length() - 1

    def order_d(j):
        owner = (j * ((1 << 16) // rows_d + 1)) >> 16
        return j + ((owner & (nx - 1)) * nz + (owner >> lx) - owner) * rows_d

    si = si_ref[...]
    owner = si >> ls
    si = (si & (rows_s - 1)) + (owner & 1) * half_s + (owner >> 1) * rows_s
    di = order_d(di_ref[...])
    ri = ri_ref[...]
    number = lax.broadcasted_iota(I32, (1, edges), 1)
    live_row = jnp.where(number < cnt_ref[...], 1.0, 0.0).astype(F32)
    columns = jnp.concatenate(
        [si.astype(F32), di.astype(F32), ri.astype(F32), live_row, jnp.zeros((4, edges), F32)], axis=0
    ).T
    si_c, di_c, ri_c = (columns[:, k : k + 1].astype(I32) for k in range(3))
    live_col = columns[:, 3:4]

    def hot(index, shape, dim):
        return jnp.where(index == lax.broadcasted_iota(I32, shape, dim), 1.0, 0.0).astype(BF16)

    def forward_z(k):
        zz = at_z(nz - k)
        arrived(("tz", k), T.at[x, zz])
        for e in range(1, nx):
            start(("tx", e, k), T.at[x, zz], T.at[x, zz], dev(xx=at_x(e)))

    def forward_y(k):
        yy = at_y(ny - k)
        arrived(("sy", k), S.at[c, yy])
        start(("sc", k), S.at[c, yy], S.at[c, yy], dev(cc=o))

    hot_r[...] = hot(ri_c, (edges, n_rel), 1)
    hot_s[...] = hot(si_c, (edges, NC * half_s), 1)
    for k in range(1, nz):
        forward_z(k)
    for k in range(1, ny):
        forward_y(k)
    hot_d[...] = hot(di_c, (edges, n_dst), 1)

    rel = rel_ref[...]
    r1, r2 = split2(rel)
    r3 = (rel - r1.astype(F32) - r2.astype(F32)).astype(BF16)
    hr = hot_r[...]
    r_v[...] = dot(hr, r1) + dot(hr, r2) + dot(hr, r3)
    ones = jnp.ones((negs, 128), BF16)
    for m in range(spans):
        nidx = order_d(ni_ref[0, m : m + 1, :])
        counts[m] = dot(hot(nidx, (n_dst, negs), 0), ones)
    cold_r[...] = hot(ri, (n_rel, edges), 0)
    cold_s[...] = hot(si, (NC * half_s, edges), 0)
    cold_d[...] = hot(di, (n_dst, edges), 0)

    for k in range(ny):
        arrived(("sc", k), S.at[o, at_y(ny - k)])
    table_s = S[...].reshape(NC * half_s, width)
    s = dot(hot_s[...], table_s)
    s_v[...] = s
    q = s * r_v[...]
    q_v[...] = q
    qb_v[...] = q.astype(BF16)

    for e in range(1, nx):
        for k in range(nz):
            arrived(("tx", e, k), T.at[at_x(nx - e), at_z(nz - k)])
    table_d = T[...].reshape(n_dst, width)
    t = dot(hot_d[...], table_d)
    t_v[...] = t
    p = jnp.sum(q_v[...] * t, axis=1, keepdims=True)
    w = -live_col * jax.nn.sigmoid(-p)
    w_v[...] = jnp.broadcast_to(w, w_v.shape)
    u32 = table_d.astype(F32)
    for m in range(spans):
        u = u32 * counts[m, :, 0:1]
        uh_v[...], ul_v[...] = split2(u)
        span = pl.ds(m * per, per)
        scores = dot_nt(qb_v[span, :], table_d)
        wn = (live_col[m * per : (m + 1) * per] * jax.nn.sigmoid(scores) * inverse).astype(BF16)
        pulled = dot(wn, uh_v[...]) + dot(wn, ul_v[...])
        g_v[span, :] = w[m * per : (m + 1) * per] * t_v[span, :] + pulled

    sg = s_v[...] * g_v[...]
    h, l = split2(sg)
    theirs = cold_r[pl.ds(o * half_r, half_r), :]
    rel_part[0] = dot(theirs, h) + dot(theirs, l)
    start(("rc",), rel_part.at[0], rel_sib, dev(cc=o))
    mine = cold_r[pl.ds(c * half_r, half_r), :]
    rel_part[1] = dot(mine, h) + dot(mine, l)

    wq = w_v[:, 0:1] * q_v[...]
    h, l = split2(wq)
    for e in [*range(nx // 2, 0, -1), *range(nx // 2 + 1, nx), 0]:
        xx = at_x(e)
        part = pl.ds(xx * part_d, part_d)
        cd = cold_d[part, :]
        total = dot(cd, h) + dot(cd, l)
        tab = T[xx].reshape(part_d, width)
        for m in range(spans):
            qb = qb_v[pl.ds(m * per, per), :]
            scores = dot_nt(tab, qb)
            wn = (live_row[:, m * per : (m + 1) * per] * jax.nn.sigmoid(scores) * inverse).astype(BF16)
            total = total + counts[m, part, 0:1] * dot(wn, qb)
        if e == 0:
            dst_part[...] = total
        else:
            dst_xs[e - 1] = total.astype(BF16).reshape(nz, rows_d, width)
            start(("dx", e), dst_xs.at[e - 1], dst_xr.at[e - 1], dev(xx=xx))

    arrived(("rc",), rel_sib)
    rel_part[1] = rel_part[1] + rel_sib[...]
    for e in range(1, nx):
        rel_xs[e - 1] = rel_part[1, pl.ds(at_x(e) * quart_r, quart_r), :].astype(BF16)
        start(("rx", e), rel_xs.at[e - 1], rel_xr.at[e - 1], dev(xx=at_x(e)))

    rg = r_v[...] * g_v[...]
    h, l = split2(rg)
    theirs = cold_s[pl.ds(o * half_s, half_s), :]
    src_part[0] = dot(theirs, h) + dot(theirs, l)
    start(("ec",), src_part.at[0], src_sib, dev(cc=o))
    mine = cold_s[pl.ds(c * half_s, half_s), :]
    src_part[1] = dot(mine, h) + dot(mine, l)

    total = rel_part[1, pl.ds(x * quart_r, quart_r), :]
    for e in range(1, nx):
        arrived(("rx", e), rel_xr.at[e - 1])
        total = total + rel_xr[e - 1].astype(F32)
    rel_zs[...] = total.reshape(rel_zs.shape)
    for k in range(1, nz):
        start(("rz", k), rel_zs.at[at_z(k)], rel_zr.at[k - 1], dev(zz=at_z(k)))

    for e in range(1, nx):
        arrived(("dx", e), dst_xr.at[e - 1])
    total = dst_part[...]
    for e in range(1, nx):
        total = total + dst_xr[e - 1].astype(F32).reshape(part_d, width)
    dst_zs[...] = total.reshape(dst_zs.shape)
    for k in range(1, nz):
        start(("dz", k), dst_zs.at[at_z(k)], dst_zr.at[k - 1], dev(zz=at_z(k)))

    arrived(("ec",), src_sib)
    src_part[1] = src_part[1] + src_sib[...]
    for k in range(1, ny):
        src_ys[k - 1] = src_part[1, pl.ds(at_y(k) * rows_s, rows_s), :].astype(BF16)
        start(("ey", k), src_ys.at[k - 1], src_yr.at[k - 1], dev(yy=at_y(k)))

    total = rel_zs[z]
    for k in range(1, nz):
        arrived(("rz", k), rel_zr.at[k - 1])
        total = total + rel_zr[k - 1]
    rel_ys[...] = total
    for k in range(1, ny):
        start(("ry", k), rel_ys, rel_yr.at[k - 1], dev(yy=at_y(k)))
    for k in range(1, ny):
        arrived(("ry", k), rel_yr.at[k - 1])
    rel_yr[ny - 1] = total
    total = jnp.zeros(total.shape, F32)
    for yy in range(ny):
        k = lax.rem(y - yy + ny, ny)
        total = total + rel_yr[lax.rem(k + ny - 1, ny)]
    RF[c, x, z] = total

    for k in range(1, nz):
        start(("bz", k), RF.at[c, x, z], RF.at[c, x, z], dev(zz=at_z(k)))
    for e in range(1, nx):
        start(("bx", e, 0), RF.at[c, x, z], RF.at[c, x, z], dev(xx=at_x(e)))
    for k in range(1, nz):
        zz = at_z(nz - k)
        arrived(("bz", k), RF.at[c, x, zz])
        for e in range(1, nx):
            start(("bx", e, k), RF.at[c, x, zz], RF.at[c, x, zz], dev(xx=at_x(e)))
    start(("bc", 0), RF.at[c, x], RF.at[c, x], dev(cc=o))

    total = dst_zs[z]
    for k in range(1, nz):
        arrived(("dz", k), dst_zr.at[k - 1])
        total = total + dst_zr[k - 1]
    out_d[...] = total
    total = src_part[1, pl.ds(y * rows_s, rows_s), :]
    for k in range(1, ny):
        arrived(("ey", k), src_yr.at[k - 1])
        total = total + src_yr[k - 1].astype(F32)
    out_s[...] = total

    for e in range(1, nx):
        xx = at_x(nx - e)
        for k in range(nz):
            arrived(("bx", e, k), RF.at[c, xx, at_z(nz - k)])
        start(("bc", e), RF.at[c, xx], RF.at[c, xx], dev(cc=o))
    out_r[pl.ds(c * half_r, half_r), :] = RF[c].reshape(half_r, width)
    for e in range(nx):
        arrived(("bc", e), RF.at[o, at_x(nx - e)])
    out_r[pl.ds(o * half_r, half_r), :] = RF[o].reshape(half_r, width)

    for d in live_copies:
        d.wait_send()
    assert len(slots) <= SEMS


def per_device(
    nz, nx, ny, src_table, dst_table, rel_diag, src_index, dst_index, rel_index, neg_index, edge_count
):
    rows_s, width = src_table.shape
    rows_d = dst_table.shape[0]
    n_rel = rel_diag.shape[0]
    edges = src_index.shape[-1]
    spans = neg_index.shape[2]
    n_src, n_dst = ny * NC * rows_s, nz * nx * rows_d
    half_r = n_rel // NC
    quart_r = half_r // nx
    eighth_r = quart_r // nz

    def v(shape, kind=F32):
        return pltpu.VMEM(shape, kind)

    return pl.pallas_call(
        functools.partial(kernel, nz, nx, ny),
        out_shape=(
            jax.ShapeDtypeStruct((rows_s, width), F32),
            jax.ShapeDtypeStruct((rows_d, width), F32),
            jax.ShapeDtypeStruct((n_rel, width), F32),
        ),
        in_specs=[pl.BlockSpec(memory_space=pltpu.VMEM)] * 8,
        out_specs=[pl.BlockSpec(memory_space=pltpu.VMEM)] * 3,
        scratch_shapes=[
            v((NC, ny, rows_s, width), BF16),
            v((nx, nz, rows_d, width), BF16),
            v((NC, nx, nz, eighth_r, width)),
            v((edges, n_src), BF16),
            v((edges, n_dst), BF16),
            v((edges, n_rel), BF16),
            v((n_src, edges), BF16),
            v((n_dst, edges), BF16),
            v((n_rel, edges), BF16),
            v((spans, n_dst, 128)),
            v((edges, width)),
            v((edges, width)),
            v((edges, width)),
            v((edges, width)),
            v((edges, width)),
            v((edges, 128)),
            v((edges, width), BF16),
            v((n_dst, width), BF16),
            v((n_dst, width), BF16),
            v((2, half_r, width)),
            v((half_r, width)),
            v((nx - 1, quart_r, width), BF16),
            v((nx - 1, quart_r, width), BF16),
            v((nz, eighth_r, width)),
            v((nz - 1, eighth_r, width)),
            v((eighth_r, width)),
            v((ny, eighth_r, width)),
            v((nx - 1, nz, rows_d, width), BF16),
            v((nz * rows_d, width)),
            v((nx - 1, nz, rows_d, width), BF16),
            v((nz, rows_d, width)),
            v((nz - 1, rows_d, width)),
            v((2, ny * rows_s, width)),
            v((ny * rows_s, width)),
            v((ny - 1, rows_s, width), BF16),
            v((ny - 1, rows_s, width), BF16),
            pltpu.SemaphoreType.DMA((SEMS,)),
            pltpu.SemaphoreType.DMA((SEMS,)),
        ],
        compiler_params=pltpu.CompilerParams(
            collective_id=0, has_side_effects=True, vmem_limit_bytes=50 * 1024 * 1024
        ),
    )(
        src_table, dst_table, rel_diag, src_index[0], dst_index[0], rel_index[0], neg_index[0], edge_count
    )


def solution(mesh):
    sizes = dict(mesh.shape)
    return jax.shard_map(
        functools.partial(per_device, sizes["src"] // NX, NX, sizes["dst"] // NC),
        mesh=mesh,
        in_specs=(
            P(("src", "dst"), None),
            P(("dst", "src"), None),
            P(),
            P("src", "dst", None),
            P("src", "dst", None),
            P("src", "dst", None),
            P("src", "dst", None, None),
            P("src", "dst"),
        ),
        out_specs=(P(("src", "dst"), None), P(("dst", "src"), None), P()),
        check_vma=False,
    )
```

time: 412 us -> 79.2 us (0.19); the launches traced: 407 us -> 79 us
  waiting for transfers between devices: 268 us -> 0 us
  Pallas kernels: 0 us -> 73.6 us
  blocking collectives: 64.9 us -> 0 us
  other arithmetic: 31.4 us -> 0 us
  local copies, waits for them, and re-layouts: 21.7 us -> 3.98 us
  between operations: 16.4 us -> 1.39 us
    psum x1 -> x0, waiting for transfers between devices: 258 us -> none  [per_device(): relation_out = lax.psum(relation_grad, ('src', 'dst'))]
    pallas_call x0 -> x1, Pallas kernels: none -> 73.6 us  [per_device(): pl.pallas_call(functools.partial(kernel, nz, nx, ny), out_shape=(jax.Shap...]
    all_gather x2 -> x0, blocking collectives: 64.9 us -> none  [the longest x1 42.3 us: per_device(): target_part = lax.all_gather(dst_table, 'src', axis=0, tiled=True)]
    scatter-add x4 -> x0, other arithmetic: 22.1 us -> none  [the longest x1 7.84 us: per_device(): target_grad = target_grad.at[flat_rows].add(flat_push)]
    gather x7 -> x0, local copies, waits for them, and re-layouts: 11.4 us -> none  [the longest x2 5.19 us: per_device(): jnp.take(target_part, negative_rows.reshape(-1), axis=0)]
    reduce_scatter x2 -> x0, waiting for transfers between devices: 10.1 us -> none  [the longest x1 10.1 us: per_device(): lax.psum_scatter(target_grad, 'src', scatter_dimension=0, tiled=True)]
    unnamed x44 -> x15, local copies, waits for them, and re-layouts: 9.16 us -> 2.78 us
  transfers between devices with their start and end apart: 3 -> 0, of which waited for: 2 -> 0; matrix products, arithmetic and copies ran while one was open for 6% -> 0% of each run, Pallas kernels for 0% -> 0%
where the time goes in v1:
time: 79.2 us; the launch traced here: 79 us
  Pallas kernels  73.6 us (93%)
  local copies, waits for them, and re-layouts  3.98 us (5%)
  between operations  1.39 us (2%)
    pallas_call x1, Pallas kernels, per_device(): pl.pallas_call(functools.partial(kernel, nz, nx, ny), out_shape=(jax.Shap...  73.6 us
    unnamed x15, local copies, waits for them, and re-layouts  2.78 us

profile of v1, /device:TPU:1, one launch (start us, length us, event | category | flops | bytes accessed | tf_op | source)
XLA Modules:
  0.0 79.0 jit_solution(1929133671504031706)
XLA Ops:
  1.3 0.0 copy-start
  1.3 0.0 copy-start.1
  1.3 0.0 copy-start.2
  1.3 0.0 copy-start.3
  1.3 0.0 copy-start.4
  1.3 0.0 copy-start.5
  1.3 1.5 %copy.11.rel_ref = f32[512,400]{1,0:T(8,128)S(1)} copy(f32[512,400]{0,1:T(8,128)} %param.10) | data formatting | bytes 1638400 | tf_op args[2]
  2.9 0.0 copy-done
  2.9 0.0 copy-done.1
  2.9 0.0 copy-done.2
  2.9 0.0 copy-done.3
  2.9 0.0 copy-done.4
  2.9 0.0 copy-done.5
  2.9 73.6 %shard_map.103 = (f32[32,400]{1,0:T(8,128)S(1)}, f32[24,400]{1,0:T(8,128)S(1)}, f32[512,400]{1,0:T(8,128)S(1)}) custom-call(bf16[32,400]{1,0:T(8,128)(2,1)S(1)} %copy-done, bf16[24,400]{1,0:T(8,128)(2,1)S(1)} %copy-done.1, f32[512,400]{1,0:T(8,128)S(1)} %copy.11.rel_ref, s32[1,512]{1,0:T(1,128)S(1)} %bitcast.5, s32[1,512]{1,0:T(1,128)S(1)} %bitcast.6, ...), custom_call_target="tpu_custom_call" | custom-call | tf_op jit(solution)/shard_map/pallas_call | solution.py:323
  76.6 1.2 %copy.12 = f32[512,400]{0,1:T(8,128)} copy(f32[512,400]{1,0:T(8,128)S(1)} %get-tuple-element.5) | data formatting | bytes 1638400 | tf_op jit(solution)/shard_map/pallas_call | solution.py:323
  77.8 0.6 copy.16
  78.4 0.6 copy.17
Async XLA Ops:
  1.3 1.6 %copy-start = (bf16[32,400]{1,0:T(8,128)(2,1)S(1)}, bf16[32,400]{1,0:T(8,128)(2,1)}, u32[]{:S(2)}) copy-start(bf16[32,400]{1,0:T(8,128)(2,1)} %src_ref.1) | copy-start | bytes 76804
  1.3 1.6 %copy-start.1 = (bf16[24,400]{1,0:T(8,128)(2,1)S(1)}, bf16[24,400]{1,0:T(8,128)(2,1)}, u32[]{:S(2)}) copy-start(bf16[24,400]{1,0:T(8,128)(2,1)} %dst_ref.1) | copy-start | bytes 57604
  1.3 1.6 %copy-start.2 = (s32[1,1,2,512]{3,2,1,0:T(2,128)S(1)}, s32[1,1,2,512]{3,2,1,0:T(2,128)}, u32[]{:S(2)}) copy-start(s32[1,1,2,512]{3,2,1,0:T(2,128)} %param.14) | copy-start | bytes 12292
  1.3 1.6 %copy-start.3 = (s32[1,1,512]{2,1,0:T(1,128)S(1)}, s32[1,1,512]{2,1,0:T(1,128)}, u32[]{:S(2)}) copy-start(s32[1,1,512]{2,1,0:T(1,128)} %param.11) | copy-start | bytes 6148
  1.3 1.6 %copy-start.4 = (s32[1,1,512]{2,1,0:T(1,128)S(1)}, s32[1,1,512]{2,1,0:T(1,128)}, u32[]{:S(2)}) copy-start(s32[1,1,512]{2,1,0:T(1,128)} %param.12) | copy-start | bytes 6148
  1.3 1.6 %copy-start.5 = (s32[1,1,512]{2,1,0:T(1,128)S(1)}, s32[1,1,512]{2,1,0:T(1,128)}, u32[]{:S(2)}) copy-start(s32[1,1,512]{2,1,0:T(1,128)} %param.13) | copy-start | bytes 6148

commit v2 on v1

v2 whole, which is shorter than its diff:
```python
import functools
import math

import jax
import jax.numpy as jnp
from jax import lax
from jax.experimental import pallas as pl
from jax.experimental.pallas import tpu as pltpu
from jax.sharding import PartitionSpec as P

F32, BF16, I32 = jnp.float32, jnp.bfloat16, jnp.int32
NX, NC = 4, 2
SEMS = 192


def dot(a, b):
    return jnp.dot(a, b, preferred_element_type=F32)


def dot_nt(a, b):
    return lax.dot_general(a, b, (((1,), (1,)), ((), ())), preferred_element_type=F32)


def split2(v):
    hi = v.astype(BF16)
    return hi, (v - hi.astype(F32)).astype(BF16)


def kernel(
    nz, nx, ny,
    src_hbm, dst_hbm, rel_hbm, si_hbm, di_hbm, ri_hbm, ni_hbm, cnt_ref,
    out_s, out_d, out_r,
    S, T, rel_v, si_ref, di_ref, ri_ref, ni_ref, hot_s, hot_d, hot_r, cold_s, cold_d, cold_r, counts, r_v, q_v, g_v, s_v, t_v, w_v, qb_v, spread,
    rel_part, rel_sib, rel_xs, rel_xr, a_first, a_got, a_mine, a_all, a_end, b_first, b_got, b_mine, b_all, b_end,
    dst_xs, dst_part, dst_xr, dst_zs, dst_zr, dst_zsb, dst_zrb,
    src_part, src_sib, src_ys, src_yr,
    send, recv, here,
):
    a, b = lax.axis_index("src"), lax.axis_index("dst")
    z, x = a // nx, lax.rem(a, nx)
    y, c = b // NC, lax.rem(b, NC)
    o = 1 - c
    rows_s, width = src_hbm.shape
    rows_d = dst_hbm.shape[0]
    half_s = ny * rows_s
    part_d = nz * rows_d
    n_dst = nx * part_d
    n_rel = rel_v.shape[1]
    half_r = n_rel // NC
    quart_r = half_r // nx
    near = sorted({1, nz - 1})
    cut = a_mine.shape[-1]
    assert ny == nz
    by_distance = sorted(range(1, nz), key=lambda k: min(k, nz - k))
    edges = si_ref.shape[-1]
    spans, negs = ni_ref.shape[-2], ni_ref.shape[-1]
    per = edges // spans
    inverse = 1.0 / math.sqrt(negs)

    def at_z(k):
        return lax.rem(z + k, nz)

    def at_x(k):
        return lax.rem(x + k, nx)

    def at_y(k):
        return lax.rem(y + k, ny)

    def dev(zz=z, xx=x, yy=y, cc=c):
        return (zz * nx + xx, yy * NC + cc)

    slots = {}
    live_copies = []

    def slot(key):
        return slots.setdefault(key, len(slots))

    def copy(key, src, dst, target):
        k = slot(key)
        return pltpu.make_async_remote_copy(
            src_ref=src, dst_ref=dst, send_sem=send.at[k], recv_sem=recv.at[k],
            device_id=target, device_id_type=pl.DeviceIdType.MESH,
        )

    def start(key, src, dst, target):
        d = copy(key, src, dst, target)
        d.start()
        live_copies.append(d)

    def arrived(key, dst):
        copy(key, dst, dst, dev(cc=o)).wait_recv()

    loads = [
        pltpu.make_async_copy(f, t, here.at[k])
        for k, (f, t) in enumerate(
            [
                (dst_hbm, T.at[x, z]), (src_hbm, S.at[c, y]), (ri_hbm, ri_ref), (si_hbm, si_ref),
                (di_hbm, di_ref), (rel_hbm, rel_v), (ni_hbm, ni_ref),
            ]
        )
    ]
    for d in loads:
        d.start()

    barrier = pltpu.get_barrier_semaphore()
    peers = [dev(cc=o)]
    peers += [dev(zz=at_z(k)) for k in range(1, nz)]
    peers += [dev(yy=at_y(k)) for k in range(1, ny)]
    peers += [dev(xx=at_x(k)) for k in range(1, nx)]
    for p in peers:
        pl.semaphore_signal(barrier, inc=1, device_id=p, device_id_type=pl.DeviceIdType.MESH)
    loads[0].wait()
    loads[1].wait()
    pl.semaphore_wait(barrier, len(peers))

    for e in range(1, nx):
        start(("tx", e, 0), T.at[x, z], T.at[x, z], dev(xx=at_x(e)))
    for k in by_distance:
        start(("tz", k), T.at[x, z], T.at[x, z], dev(zz=at_z(k)))
    for k in range(1, ny):
        start(("sy", k), S.at[c, y], S.at[c, y], dev(yy=at_y(k)))
    start(("sc", 0), S.at[c, y], S.at[c, y], dev(cc=o))

    for d in loads[2:]:
        d.wait()
    lx, ls = nx.bit_length() - 1, rows_s.bit_length() - 1

    def order_d(j):
        owner = (j * ((1 << 16) // rows_d + 1)) >> 16
        return j + ((owner & (nx - 1)) * nz + (owner >> lx) - owner) * rows_d

    si = si_ref[...]
    owner = si >> ls
    si = (si & (rows_s - 1)) + (owner & 1) * half_s + (owner >> 1) * rows_s
    di = order_d(di_ref[...])
    ri = ri_ref[...]
    number = lax.broadcasted_iota(I32, (1, edges), 1)
    live_row = jnp.where(number < cnt_ref[...], 1.0, 0.0).astype(F32)
    columns = jnp.concatenate(
        [si.astype(F32), di.astype(F32), ri.astype(F32), live_row, jnp.zeros((4, edges), F32)], axis=0
    ).T
    si_c, di_c, ri_c = (columns[:, k : k + 1].astype(I32) for k in range(3))
    live_col = columns[:, 3:4]

    def hot(index, shape, dim):
        return jnp.where(index == lax.broadcasted_iota(I32, shape, dim), 1.0, 0.0).astype(BF16)

    def forward_z(k):
        zz = at_z(nz - k)
        arrived(("tz", k), T.at[x, zz])
        for e in range(1, nx):
            start(("tx", e, k), T.at[x, zz], T.at[x, zz], dev(xx=at_x(e)))

    def forward_x(e):
        xx = at_x(nx - e)
        arrived(("tx", e, 0), T.at[xx, z])
        for k in near:
            start(("tx", e, k), T.at[xx, z], T.at[xx, z], dev(zz=at_z(k)))

    def forward_y(k):
        yy = at_y(ny - k)
        arrived(("sy", k), S.at[c, yy])
        start(("sc", k), S.at[c, yy], S.at[c, yy], dev(cc=o))

    hot_r[...] = hot(ri_c, (edges, n_rel), 1)
    hot_s[...] = hot(si_c, (edges, NC * half_s), 1)
    forward_x(1)
    forward_x(nx - 1) if nx > 2 else None
    far = [k for k in by_distance if k not in near]
    for k in far[:2]:
        forward_z(k)
    for e in range(2, nx - 1):
        forward_x(e)
    for k in far[2:]:
        forward_z(k)
    for k in range(1, ny):
        forward_y(k)
    for e in range(nx):
        hot_d[e] = hot(di_c - at_x(nx - e) * part_d, (edges, part_d), 1)

    rel = rel_v[...]
    r1, r2 = split2(rel)
    r3 = (rel - r1.astype(F32) - r2.astype(F32)).astype(BF16)
    hr = hot_r[...]
    r_v[...] = dot_nt(hr, r1) + dot_nt(hr, r2) + dot_nt(hr, r3)
    ones = jnp.ones((negs, 128), BF16)
    for m in range(spans):
        nidx = order_d(ni_ref[0, m : m + 1, :])
        counts[m] = dot(hot(nidx, (n_dst, negs), 0), ones)
    cold_r[...] = hot(ri, (n_rel, edges), 0)
    cold_s[...] = hot(si, (NC * half_s, edges), 0)
    cold_d[...] = hot(di, (n_dst, edges), 0)

    for k in range(ny):
        arrived(("sc", k), S.at[o, at_y(ny - k)])
    table_s = S[...].reshape(NC * half_s, width)
    s = dot(hot_s[...], table_s)
    s_v[...] = s
    q = s * r_v[...]
    q_v[...] = q
    qb_v[...] = q.astype(BF16)

    def weights(live, scores):
        return (live * jax.nn.sigmoid(scores) * inverse).astype(BF16)

    def spread_terms(xx):
        part = pl.ds(xx * part_d, part_d)
        tab = T[xx].reshape(part_d, width)
        total = jnp.zeros((part_d, width), F32)
        for m in range(spans):
            qb = qb_v[pl.ds(m * per, per), :]
            wn = weights(live_row[:, m * per : (m + 1) * per], dot_nt(tab, qb))
            total = total + counts[m, part, 0:1] * dot(wn, qb)
        spread[xx] = total

    arrivals = [0, *sorted(range(1, nx), key=lambda e: min(e, nx - e))]
    for n, e in enumerate(arrivals):
        xx = at_x(nx - e)
        if e == 0:
            for k in near:
                arrived(("tz", k), T.at[x, at_z(nz - k)])
        else:
            for k in range(1, nz):
                arrived(("tx", e, k), T.at[xx, at_z(nz - k)])
        tab = T[xx].reshape(part_d, width)
        t = dot(hot_d[e], tab)
        t_v[...] = t if n == 0 else t_v[...] + t
        tab_f = tab.astype(F32)
        for m in range(spans):
            span = pl.ds(m * per, per)
            uh, ul = split2(tab_f * counts[m, pl.ds(xx * part_d, part_d), 0:1])
            wn = weights(live_col[m * per : (m + 1) * per], dot_nt(qb_v[span, :], tab))
            pulled = dot(wn, uh) + dot(wn, ul)
            g_v[span, :] = pulled if n == 0 else g_v[span, :] + pulled
        if n < nx - 1:
            spread_terms(xx)
    p = jnp.sum(q_v[...] * t_v[...], axis=1, keepdims=True)
    w = -live_col * jax.nn.sigmoid(-p)
    w_v[...] = jnp.broadcast_to(w, w_v.shape)
    g_v[...] = w * t_v[...] + g_v[...]

    sg = s_v[...] * g_v[...]
    h, l = split2(sg)
    theirs = cold_r[pl.ds(o * half_r, half_r), :]
    rel_part[0] = dot(theirs, h) + dot(theirs, l)
    order_x = [*range(nx // 2, 0, -1), *range(nx // 2 + 1, nx)]

    def quarter(e):
        return pl.ds(at_x(e) * quart_r, quart_r)

    for e in [*order_x, 0]:
        start(("rc", e), rel_part.at[0, quarter(e)], rel_sib.at[quarter(e)], dev(cc=o))
    mine = cold_r[pl.ds(c * half_r, half_r), :]
    rel_part[1] = dot(mine, h) + dot(mine, l)

    for e in order_x:
        arrived(("rc", e), rel_sib.at[quarter(e)])
        rel_xs[e - 1] = (rel_part[1, quarter(e), :] + rel_sib[quarter(e), :]).astype(BF16)
        start(("rx", e), rel_xs.at[e - 1], rel_xr.at[e - 1], dev(xx=at_x(e)))

    wh, wl = split2(w_v[:, 0:1] * q_v[...])

    def target_terms(e):
        xx = at_x(e)
        cd = cold_d[pl.ds(xx * part_d, part_d), :]
        total = dot(cd, wh) + dot(cd, wl) + spread[xx]
        if e == 0:
            dst_part[...] = total
        else:
            dst_xs[e - 1] = total.astype(BF16).reshape(nz, rows_d, width)
            start(("dx", e), dst_xs.at[e - 1], dst_xr.at[e - 1], dev(xx=xx))

    for e in range(1, nx):
        if e == nx // 2:
            spread_terms(at_x(nx - arrivals[-1]))
        target_terms(e)

    sh, sl = split2(r_v[...] * g_v[...])
    theirs = cold_s[pl.ds(o * half_s, half_s), :]
    src_part[0] = dot(theirs, sh) + dot(theirs, sl)
    start(("ec",), src_part.at[0], src_sib, dev(cc=o))

    arrived(("rc", 0), rel_sib.at[quarter(0)])
    total = rel_part[1, quarter(0), :] + rel_sib[quarter(0), :]
    for e in range(1, nx):
        arrived(("rx", e), rel_xr.at[e - 1])
        total = total + rel_xr[e - 1].astype(F32)
    a_first[...] = total[:, :cut].reshape(a_first.shape)
    b_first[...] = total[:, cut:].reshape(b_first.shape)
    for k in range(1, ny):
        start(("ay", k), a_first.at[at_y(k)], a_got.at[k - 1], dev(yy=at_y(k)))
        start(("bz", k), b_first.at[at_z(k)], b_got.at[k - 1], dev(zz=at_z(k)))

    mine = cold_s[pl.ds(c * half_s, half_s), :]
    src_part[1] = dot(mine, sh) + dot(mine, sl)
    arrived(("ec",), src_sib)
    src_part[1] = src_part[1] + src_sib[...]
    for k in range(1, ny):
        src_ys[k - 1] = src_part[1, pl.ds(at_y(k) * rows_s, rows_s), :].astype(BF16)
        start(("ey", k), src_ys.at[k - 1], src_yr.at[k - 1], dev(yy=at_y(k)))
    target_terms(0)

    ta, tb = a_first[y], b_first[z]
    for k in range(1, ny):
        arrived(("ay", k), a_got.at[k - 1])
        ta = ta + a_got[k - 1]
    a_mine[...] = ta
    for k in range(1, nz):
        start(("az", k), a_mine, a_all.at[k - 1], dev(zz=at_z(k)))
    for k in range(1, nz):
        arrived(("bz", k), b_got.at[k - 1])
        tb = tb + b_got[k - 1]
    b_mine[...] = tb
    for k in range(1, ny):
        start(("by", k), b_mine, b_all.at[k - 1], dev(yy=at_y(k)))
    a_all[nz - 1] = ta
    b_all[ny - 1] = tb

    for e in range(1, nx):
        arrived(("dx", e), dst_xr.at[e - 1])
    total = dst_part[...]
    for e in range(1, nx):
        total = total + dst_xr[e - 1].astype(F32).reshape(part_d, width)
    dst_zs[...] = total.reshape(dst_zs.shape)
    dst_zsb[...] = dst_zs[...].astype(BF16)

    for k in range(1, nz):
        arrived(("az", k), a_all.at[k - 1])
    total = jnp.zeros(a_mine.shape, F32)
    for zz in range(nz):
        total = total + a_all[lax.rem(z - zz + 2 * nz - 1, nz)]
    a_end[c, x, y] = total
    for k in range(1, ny):
        arrived(("by", k), b_all.at[k - 1])
    total = jnp.zeros(b_mine.shape, F32)
    for yy in range(ny):
        total = total + b_all[lax.rem(y - yy + 2 * ny - 1, ny)]
    b_end[c, x, z] = total

    def along_y(k):
        return dev(yy=at_y(k))

    def along_z(k):
        return dev(zz=at_z(k))

    routes = [("A", a_end, at_y, along_y), ("B", b_end, at_z, along_z)]
    for e in range(1, nx):
        for name, end, at, along in routes:
            start((name + "x", e, 0), end.at[c, x, at(0)], end.at[c, x, at(0)], dev(xx=at_x(e)))
    for k in by_distance:
        for name, end, at, along in routes:
            start((name, k), end.at[c, x, at(0)], end.at[c, x, at(0)], along(k))

    def distant(k):
        return 8 * min(k, nz - k) >= 3 * nz

    for k in by_distance[::-1]:
        if distant(k):
            start(("dz", k), dst_zsb.at[at_z(k)], dst_zrb.at[k - 1], dev(zz=at_z(k)))
        else:
            start(("dz", k), dst_zs.at[at_z(k)], dst_zr.at[k - 1], dev(zz=at_z(k)))

    def back_x(e):
        for name, end, at, along in routes:
            block = end.at[c, at_x(nx - e), at(0)]
            arrived((name + "x", e, 0), block)
            for k in near:
                start((name + "x", e, k), block, block, along(k))

    def back_line(k):
        for name, end, at, along in routes:
            block = end.at[c, x, at(nz - k)]
            arrived((name, k), block)
            if k not in near:
                for e in range(1, nx):
                    start((name + "x", e, k), block, block, dev(xx=at_x(e)))

    back_x(1)
    back_x(nx - 1) if nx > 2 else None
    for k in far[:2]:
        back_line(k)
    for e in range(2, nx - 1):
        back_x(e)
    for k in [*far[2:], *near]:
        back_line(k)
    for name, end, at, along in routes:
        start((name + "c", 0), end.at[c, x], end.at[c, x], dev(cc=o))

    for e in range(1, nx):
        xx = at_x(nx - e)
        for name, end, at, along in routes:
            for k in range(1, nz):
                arrived((name + "x", e, k), end.at[c, xx, at(nz - k)])
            start((name + "c", e), end.at[c, xx], end.at[c, xx], dev(cc=o))

    def turn(half):
        lanes = pl.ds(pl.multiple_of(half * half_r, half_r), half_r)
        out_r[0:cut, lanes] = a_end[half].reshape(half_r, cut).T
        out_r[cut:, lanes] = b_end[half].reshape(half_r, width - cut).T

    turn(c)

    total = dst_zs[z]
    for k in range(1, nz):
        if distant(k):
            arrived(("dz", k), dst_zrb.at[k - 1])
            total = total + dst_zrb[k - 1].astype(F32)
        else:
            arrived(("dz", k), dst_zr.at[k - 1])
            total = total + dst_zr[k - 1]
    out_d[...] = total
    total = src_part[1, pl.ds(y * rows_s, rows_s), :]
    for k in range(1, ny):
        arrived(("ey", k), src_yr.at[k - 1])
        total = total + src_yr[k - 1].astype(F32)
    out_s[...] = total

    for e in range(nx):
        for name, end, at, along in routes:
            arrived((name + "c", e), end.at[o, at_x(nx - e)])
    turn(o)
    for d in live_copies:
        d.wait_send()
    assert len(slots) <= SEMS


def per_device(
    nz, nx, ny, src_table, dst_table, rel_diag, src_index, dst_index, rel_index, neg_index, edge_count
):
    rows_s, width = src_table.shape
    rows_d = dst_table.shape[0]
    n_rel = rel_diag.shape[0]
    rel_turned = rel_diag.T
    edges = src_index.shape[-1]
    spans, negs = neg_index.shape[2:]
    n_src, n_dst = ny * NC * rows_s, nz * nx * rows_d
    half_r = n_rel // NC
    quart_r = half_r // nx
    eighth_r = quart_r // ny
    cut = 256

    def v(shape, kind=F32):
        return pltpu.VMEM(shape, kind)

    grads = pl.pallas_call(
        functools.partial(kernel, nz, nx, ny),
        out_shape=(
            pltpu.VMEM((rows_s, width), F32),
            pltpu.VMEM((rows_d, width), F32),
            pltpu.VMEM((width, n_rel), F32),
        ),
        in_specs=[pl.BlockSpec(memory_space=pltpu.HBM)] * 7 + [pl.BlockSpec(memory_space=pltpu.VMEM)],
        out_specs=[pl.BlockSpec(memory_space=pltpu.VMEM)] * 3,
        scratch_shapes=[
            v((NC, ny, rows_s, width), BF16),
            v((nx, nz, rows_d, width), BF16),
            v((width, n_rel)),
            v((1, edges), I32),
            v((1, edges), I32),
            v((1, edges), I32),
            v((1, spans, negs), I32),
            v((edges, n_src), BF16),
            v((nx, edges, nz * rows_d), BF16),
            v((edges, n_rel), BF16),
            v((n_src, edges), BF16),
            v((n_dst, edges), BF16),
            v((n_rel, edges), BF16),
            v((spans, n_dst, 128)),
            v((edges, width)),
            v((edges, width)),
            v((edges, width)),
            v((edges, width)),
            v((edges, width)),
            v((edges, 128)),
            v((edges, width), BF16),
            v((nx, nz * rows_d, width)),
            v((2, half_r, width)),
            v((half_r, width)),
            v((nx - 1, quart_r, width), BF16),
            v((nx - 1, quart_r, width), BF16),
            *(
                v((*lead, eighth_r, wide))
                for wide in (cut, width - cut)
                for lead in ((ny,), (ny - 1,), (), (nz,), (NC, nx, ny))
            ),
            v((nx - 1, nz, rows_d, width), BF16),
            v((nz * rows_d, width)),
            v((nx - 1, nz, rows_d, width), BF16),
            v((nz, rows_d, width)),
            v((nz - 1, rows_d, width)),
            v((nz, rows_d, width), BF16),
            v((nz - 1, rows_d, width), BF16),
            v((2, ny * rows_s, width)),
            v((ny * rows_s, width)),
            v((ny - 1, rows_s, width), BF16),
            v((ny - 1, rows_s, width), BF16),
            pltpu.SemaphoreType.DMA((SEMS,)),
            pltpu.SemaphoreType.DMA((SEMS,)),
            pltpu.SemaphoreType.DMA((7,)),
        ],
        compiler_params=pltpu.CompilerParams(
            collective_id=0, has_side_effects=True, vmem_limit_bytes=50 * 1024 * 1024
        ),
    )(
        *(
            pltpu.with_memory_space_constraint(t, pltpu.HBM)
            for t in (src_table, dst_table, rel_turned, src_index[0], dst_index[0], rel_index[0], neg_index[0])
        ),
        edge_count,
    )
    return grads[0], grads[1], grads[2].T


def solution(mesh):
    sizes = dict(mesh.shape)
    return jax.shard_map(
        functools.partial(per_device, sizes["src"] // NX, NX, sizes["dst"] // NC),
        mesh=mesh,
        in_specs=(
            P(("src", "dst"), None),
            P(("dst", "src"), None),
            P(),
            P("src", "dst", None),
            P("src", "dst", None),
            P("src", "dst", None),
            P("src", "dst", None, None),
            P("src", "dst"),
        ),
        out_specs=(P(("src", "dst"), None), P(("dst", "src"), None), P()),
        check_vma=False,
    )
```

time: 79.2 us -> 70.2 us (0.89)
  Pallas kernels: 73.6 us -> 66.6 us
  local copies, waits for them, and re-layouts: 3.98 us -> 2.14 us
    pallas_call x1, Pallas kernels: 73.6 us -> 66.6 us  [per_device(): pl.pallas_call(functools.partial(kernel, nz, nx, ny), out_shape=(pltpu.VM...]
    pallas_call x1 -> x0, local copies, waits for them, and re-layouts: 1.2 us -> none  [per_device(): pl.pallas_call(functools.partial(kernel, nz, nx, ny), out_shape=(jax.Shap...]
    unnamed x15 -> x3, local copies, waits for them, and re-layouts: 2.78 us -> 2.14 us
where the time goes in v2:
time: 70.2 us; the launch traced here: 70 us
  Pallas kernels  66.6 us (95%)
  local copies, waits for them, and re-layouts  2.14 us (3%)
  between operations  1.29 us (2%)
    pallas_call x1, Pallas kernels, per_device(): pl.pallas_call(functools.partial(kernel, nz, nx, ny), out_shape=(pltpu.VM...  66.6 us
    unnamed x3, local copies, waits for them, and re-layouts  2.14 us

profile of v2, /device:TPU:1, one launch (start us, length us, event | category | flops | bytes accessed | tf_op | source)
XLA Modules:
  0.0 70.0 jit_solution(9922306834515987003)
XLA Ops:
  1.3 66.6 %shard_map.103 = (f32[32,400]{1,0:T(8,128)S(1)}, f32[24,400]{1,0:T(8,128)S(1)}, f32[400,512]{1,0:T(8,128)S(1)}) custom-call(bf16[32,400]{1,0:T(8,128)(2,1)} %src_hbm.1, bf16[24,400]{1,0:T(8,128)(2,1)} %dst_hbm.1, f32[400,512]{1,0:T(8,128)} %bitcast.7, s32[1,512]{1,0:T(1,128)} %bitcast.9, s32[1,512]{1,0:T(1,128)} %bitcast.10, s32[1,512]{1,0:T(1,128)} %bitcast.11, ...), custom_call_target="tpu_custom_call" | custom-call | tf_op jit(solution)/shard_map/pallas_call | solution.py:445
  67.9 0.6 copy.14
  68.5 0.6 copy.15
  69.1 0.9 %copy.16 = f32[512,400]{0,1:T(8,128)} copy(f32[512,400]{0,1:T(8,128)S(1)} %bitcast.6) | data formatting | bytes 1638400

commit v3 on v2

--- a/solution.py
+++ b/solution.py
@@ -115,7 +115,8 @@
 
     for e in range(1, nx):
         start(("tx", e, 0), T.at[x, z], T.at[x, z], dev(xx=at_x(e)))
-    for k in by_distance:
+    far = [k for k in by_distance if k not in near]
+    for k in [*far, *near]:
         start(("tz", k), T.at[x, z], T.at[x, z], dev(zz=at_z(k)))
     for k in range(1, ny):
         start(("sy", k), S.at[c, y], S.at[c, y], dev(yy=at_y(k)))
@@ -166,7 +167,6 @@
     hot_s[...] = hot(si_c, (edges, NC * half_s), 1)
     forward_x(1)
     forward_x(nx - 1) if nx > 2 else None
-    far = [k for k in by_distance if k not in near]
     for k in far[:2]:
         forward_z(k)
     for e in range(2, nx - 1):
@@ -297,7 +297,6 @@
     src_part[1] = src_part[1] + src_sib[...]
     for k in range(1, ny):
         src_ys[k - 1] = src_part[1, pl.ds(at_y(k) * rows_s, rows_s), :].astype(BF16)
-        start(("ey", k), src_ys.at[k - 1], src_yr.at[k - 1], dev(yy=at_y(k)))
     target_terms(0)
 
     ta, tb = a_first[y], b_first[z]
@@ -316,6 +315,9 @@
     a_all[nz - 1] = ta
     b_all[ny - 1] = tb
 
+    for k in range(1, ny):
+        start(("ey", k), src_ys.at[k - 1], src_yr.at[k - 1], dev(yy=at_y(k)))
+
     for e in range(1, nx):
         arrived(("dx", e), dst_xr.at[e - 1])
     total = dst_part[...]
@@ -323,6 +325,15 @@
         total = total + dst_xr[e - 1].astype(F32).reshape(part_d, width)
     dst_zs[...] = total.reshape(dst_zs.shape)
     dst_zsb[...] = dst_zs[...].astype(BF16)
+
+    def distant(k):
+        return 8 * min(k, nz - k) >= 3 * nz
+
+    for k in by_distance[::-1]:
+        if distant(k):
+            start(("dz", k), dst_zsb.at[at_z(k)], dst_zrb.at[k - 1], dev(zz=at_z(k)))
+        else:
+            start(("dz", k), dst_zs.at[at_z(k)], dst_zr.at[k - 1], dev(zz=at_z(k)))
 
     for k in range(1, nz):
         arrived(("az", k), a_all.at[k - 1])
@@ -344,21 +355,17 @@
         return dev(zz=at_z(k))
 
     routes = [("A", a_end, at_y, along_y), ("B", b_end, at_z, along_z)]
+    def back_own(k):
+        for name, end, at, along in routes:
+            start((name, k), end.at[c, x, at(0)], end.at[c, x, at(0)], along(k))
+
+    for k in far[::-1]:
+        back_own(k)
     for e in range(1, nx):
         for name, end, at, along in routes:
             start((name + "x", e, 0), end.at[c, x, at(0)], end.at[c, x, at(0)], dev(xx=at_x(e)))
-    for k in by_distance:
-        for name, end, at, along in routes:
-            start((name, k), end.at[c, x, at(0)], end.at[c, x, at(0)], along(k))
-
-    def distant(k):
-        return 8 * min(k, nz - k) >= 3 * nz
-
-    for k in by_distance[::-1]:
-        if distant(k):
-            start(("dz", k), dst_zsb.at[at_z(k)], dst_zrb.at[k - 1], dev(zz=at_z(k)))
-        else:
-            start(("dz", k), dst_zs.at[at_z(k)], dst_zr.at[k - 1], dev(zz=at_z(k)))
+    for k in near:
+        back_own(k)
 
     def back_x(e):
         for name, end, at, along in routes:

time: 70.2 us -> 71.1 us (1.013)
  Pallas kernels: 66.6 us -> 67.5 us
    pallas_call x1, Pallas kernels: 66.6 us -> 67.5 us  [per_device(): pl.pallas_call(functools.partial(kernel, nz, nx, ny), out_shape=(pltpu.VM...]
where the time goes in v3:
time: 71.1 us; the launch traced here: 71 us
  Pallas kernels  67.5 us (95%)
  local copies, waits for them, and re-layouts  2.14 us (3%)
  between operations  1.29 us (2%)
    pallas_call x1, Pallas kernels, per_device(): pl.pallas_call(functools.partial(kernel, nz, nx, ny), out_shape=(pltpu.VM...  67.5 us
    unnamed x3, local copies, waits for them, and re-layouts  2.14 us

profile of v3, /device:TPU:1, one launch (start us, length us, event | category | flops | bytes accessed | tf_op | source)
XLA Modules:
  0.0 71.0 jit_solution(4697001472015038727)
XLA Ops:
  1.3 67.5 %shard_map.103 = (f32[32,400]{1,0:T(8,128)S(1)}, f32[24,400]{1,0:T(8,128)S(1)}, f32[400,512]{1,0:T(8,128)S(1)}) custom-call(bf16[32,400]{1,0:T(8,128)(2,1)} %src_hbm.1, bf16[24,400]{1,0:T(8,128)(2,1)} %dst_hbm.1, f32[400,512]{1,0:T(8,128)} %bitcast.7, s32[1,512]{1,0:T(1,128)} %bitcast.9, s32[1,512]{1,0:T(1,128)} %bitcast.10, s32[1,512]{1,0:T(1,128)} %bitcast.11, ...), custom_call_target="tpu_custom_call" | custom-call | tf_op jit(solution)/shard_map/pallas_call | solution.py:452
  68.8 0.6 copy.14
  69.5 0.6 copy.15
  70.1 0.9 %copy.16 = f32[512,400]{0,1:T(8,128)} copy(f32[512,400]{0,1:T(8,128)S(1)} %bitcast.6) | data formatting | bytes 1638400

commit v4 on v3

--- a/solution.py
+++ b/solution.py
@@ -32,7 +32,7 @@
     out_s, out_d, out_r,
     S, T, rel_v, si_ref, di_ref, ri_ref, ni_ref, hot_s, hot_d, hot_r, cold_s, cold_d, cold_r, counts, r_v, q_v, g_v, s_v, t_v, w_v, qb_v, spread,
     rel_part, rel_sib, rel_xs, rel_xr, a_first, a_got, a_mine, a_all, a_end, b_first, b_got, b_mine, b_all, b_end,
-    dst_xs, dst_part, dst_xr, dst_zs, dst_zr, dst_zsb, dst_zrb,
+    dst_xs, dst_part, dst_xr, dst_zs, dst_zsb, dst_zrb,
     src_part, src_sib, src_ys, src_yr,
     send, recv, here,
 ):
@@ -232,7 +232,7 @@
             wn = weights(live_col[m * per : (m + 1) * per], dot_nt(qb_v[span, :], tab))
             pulled = dot(wn, uh) + dot(wn, ul)
             g_v[span, :] = pulled if n == 0 else g_v[span, :] + pulled
-        if n < nx - 1:
+        if n == 0:
             spread_terms(xx)
     p = jnp.sum(q_v[...] * t_v[...], axis=1, keepdims=True)
     w = -live_col * jax.nn.sigmoid(-p)
@@ -271,8 +271,7 @@
             start(("dx", e), dst_xs.at[e - 1], dst_xr.at[e - 1], dev(xx=xx))
 
     for e in range(1, nx):
-        if e == nx // 2:
-            spread_terms(at_x(nx - arrivals[-1]))
+        spread_terms(at_x(e))
         target_terms(e)
 
     sh, sl = split2(r_v[...] * g_v[...])
@@ -318,23 +317,6 @@
     for k in range(1, ny):
         start(("ey", k), src_ys.at[k - 1], src_yr.at[k - 1], dev(yy=at_y(k)))
 
-    for e in range(1, nx):
-        arrived(("dx", e), dst_xr.at[e - 1])
-    total = dst_part[...]
-    for e in range(1, nx):
-        total = total + dst_xr[e - 1].astype(F32).reshape(part_d, width)
-    dst_zs[...] = total.reshape(dst_zs.shape)
-    dst_zsb[...] = dst_zs[...].astype(BF16)
-
-    def distant(k):
-        return 8 * min(k, nz - k) >= 3 * nz
-
-    for k in by_distance[::-1]:
-        if distant(k):
-            start(("dz", k), dst_zsb.at[at_z(k)], dst_zrb.at[k - 1], dev(zz=at_z(k)))
-        else:
-            start(("dz", k), dst_zs.at[at_z(k)], dst_zr.at[k - 1], dev(zz=at_z(k)))
-
     for k in range(1, nz):
         arrived(("az", k), a_all.at[k - 1])
     total = jnp.zeros(a_mine.shape, F32)
@@ -366,6 +348,17 @@
             start((name + "x", e, 0), end.at[c, x, at(0)], end.at[c, x, at(0)], dev(xx=at_x(e)))
     for k in near:
         back_own(k)
+
+    for e in range(1, nx):
+        arrived(("dx", e), dst_xr.at[e - 1])
+    total = dst_part[...]
+    for e in range(1, nx):
+        total = total + dst_xr[e - 1].astype(F32).reshape(part_d, width)
+    dst_zs[...] = total.reshape(dst_zs.shape)
+    dst_zsb[...] = dst_zs[...].astype(BF16)
+
+    for k in by_distance[::-1]:
+        start(("dz", k), dst_zsb.at[at_z(k)], dst_zrb.at[k - 1], dev(zz=at_z(k)))
 
     def back_x(e):
         for name, end, at, along in routes:
@@ -409,12 +402,8 @@
 
     total = dst_zs[z]
     for k in range(1, nz):
-        if distant(k):
-            arrived(("dz", k), dst_zrb.at[k - 1])
-            total = total + dst_zrb[k - 1].astype(F32)
-        else:
-            arrived(("dz", k), dst_zr.at[k - 1])
-            total = total + dst_zr[k - 1]
+        arrived(("dz", k), dst_zrb.at[k - 1])
+        total = total + dst_zrb[k - 1].astype(F32)
     out_d[...] = total
     total = src_part[1, pl.ds(y * rows_s, rows_s), :]
     for k in range(1, ny):
@@ -494,7 +483,6 @@
             v((nz * rows_d, width)),
             v((nx - 1, nz, rows_d, width), BF16),
             v((nz, rows_d, width)),
-            v((nz - 1, rows_d, width)),
             v((nz, rows_d, width), BF16),
             v((nz - 1, rows_d, width), BF16),
             v((2, ny * rows_s, width)),

time: 71.1 us -> 66.5 us (0.935)
  Pallas kernels: 67.5 us -> 62.9 us
    pallas_call x1, Pallas kernels: 67.5 us -> 62.9 us  [per_device(): pl.pallas_call(functools.partial(kernel, nz, nx, ny), out_shape=(pltpu.VM...]
where the time goes in v4:
time: 66.5 us; the launch traced here: 66.3 us
  Pallas kernels  62.9 us (95%)
  local copies, waits for them, and re-layouts  2.14 us (3%)
  between operations  1.29 us (2%)
    pallas_call x1, Pallas kernels, per_device(): pl.pallas_call(functools.partial(kernel, nz, nx, ny), out_shape=(pltpu.VM...  62.9 us
    unnamed x3, local copies, waits for them, and re-layouts  2.14 us

profile of v4, /device:TPU:1, one launch (start us, length us, event | category | flops | bytes accessed | tf_op | source)
XLA Modules:
  0.0 66.3 jit_solution(5963847743136191785)
XLA Ops:
  1.3 62.9 %shard_map.103 = (f32[32,400]{1,0:T(8,128)S(1)}, f32[24,400]{1,0:T(8,128)S(1)}, f32[400,512]{1,0:T(8,128)S(1)}) custom-call(bf16[32,400]{1,0:T(8,128)(2,1)} %src_hbm.1, bf16[24,400]{1,0:T(8,128)(2,1)} %dst_hbm.1, f32[400,512]{1,0:T(8,128)} %bitcast.7, s32[1,512]{1,0:T(1,128)} %bitcast.9, s32[1,512]{1,0:T(1,128)} %bitcast.10, s32[1,512]{1,0:T(1,128)} %bitcast.11, ...), custom_call_target="tpu_custom_call" | custom-call | tf_op jit(solution)/shard_map/pallas_call | solution.py:441
  64.2 0.6 copy.14
  64.8 0.6 copy.15
  65.4 0.9 %copy.16 = f32[512,400]{0,1:T(8,128)} copy(f32[512,400]{0,1:T(8,128)S(1)} %bitcast.6) | data formatting | bytes 1638400

commit v5 on v4

--- a/solution.py
+++ b/solution.py
@@ -169,27 +169,25 @@
     forward_x(nx - 1) if nx > 2 else None
     for k in far[:2]:
         forward_z(k)
-    for e in range(2, nx - 1):
-        forward_x(e)
-    for k in far[2:]:
-        forward_z(k)
-    for k in range(1, ny):
-        forward_y(k)
-    for e in range(nx):
-        hot_d[e] = hot(di_c - at_x(nx - e) * part_d, (edges, part_d), 1)
-
     rel = rel_v[...]
     r1, r2 = split2(rel)
     r3 = (rel - r1.astype(F32) - r2.astype(F32)).astype(BF16)
     hr = hot_r[...]
     r_v[...] = dot_nt(hr, r1) + dot_nt(hr, r2) + dot_nt(hr, r3)
+    for e in range(2, nx - 1):
+        forward_x(e)
+    for k in far[2:]:
+        forward_z(k)
+    for k in range(1, ny):
+        forward_y(k)
+    for e in range(nx):
+        hot_d[e] = hot(di_c - at_x(nx - e) * part_d, (edges, part_d), 1)
+
     ones = jnp.ones((negs, 128), BF16)
     for m in range(spans):
         nidx = order_d(ni_ref[0, m : m + 1, :])
         counts[m] = dot(hot(nidx, (n_dst, negs), 0), ones)
     cold_r[...] = hot(ri, (n_rel, edges), 0)
-    cold_s[...] = hot(si, (NC * half_s, edges), 0)
-    cold_d[...] = hot(di, (n_dst, edges), 0)
 
     for k in range(ny):
         arrived(("sc", k), S.at[o, at_y(ny - k)])
@@ -258,6 +256,7 @@
         rel_xs[e - 1] = (rel_part[1, quarter(e), :] + rel_sib[quarter(e), :]).astype(BF16)
         start(("rx", e), rel_xs.at[e - 1], rel_xr.at[e - 1], dev(xx=at_x(e)))
 
+    cold_d[...] = hot(di, (n_dst, edges), 0)
     wh, wl = split2(w_v[:, 0:1] * q_v[...])
 
     def target_terms(e):
@@ -274,6 +273,7 @@
         spread_terms(at_x(e))
         target_terms(e)
 
+    cold_s[...] = hot(si, (NC * half_s, edges), 0)
     sh, sl = split2(r_v[...] * g_v[...])
     theirs = cold_s[pl.ds(o * half_s, half_s), :]
     src_part[0] = dot(theirs, sh) + dot(theirs, sl)

time: 66.5 us -> 67.2 us (1.011)
  Pallas kernels: 62.9 us -> 63.6 us
    pallas_call x1, Pallas kernels: 62.9 us -> 63.6 us  [per_device(): pl.pallas_call(functools.partial(kernel, nz, nx, ny), out_shape=(pltpu.VM...]
where the time goes in v5:
time: 67.2 us; the launch traced here: 67.1 us
  Pallas kernels  63.6 us (95%)
  local copies, waits for them, and re-layouts  2.14 us (3%)
  between operations  1.29 us (2%)
    pallas_call x1, Pallas kernels, per_device(): pl.pallas_call(functools.partial(kernel, nz, nx, ny), out_shape=(pltpu.VM...  63.6 us
    unnamed x3, local copies, waits for them, and re-layouts  2.14 us

profile of v5, /device:TPU:1, one launch (start us, length us, event | category | flops | bytes accessed | tf_op | source)
XLA Modules:
  0.0 67.1 jit_solution(3032363702276132766)
XLA Ops:
  1.3 63.6 %shard_map.103 = (f32[32,400]{1,0:T(8,128)S(1)}, f32[24,400]{1,0:T(8,128)S(1)}, f32[400,512]{1,0:T(8,128)S(1)}) custom-call(bf16[32,400]{1,0:T(8,128)(2,1)} %src_hbm.1, bf16[24,400]{1,0:T(8,128)(2,1)} %dst_hbm.1, f32[400,512]{1,0:T(8,128)} %bitcast.7, s32[1,512]{1,0:T(1,128)} %bitcast.9, s32[1,512]{1,0:T(1,128)} %bitcast.10, s32[1,512]{1,0:T(1,128)} %bitcast.11, ...), custom_call_target="tpu_custom_call" | custom-call | tf_op jit(solution)/shard_map/pallas_call | solution.py:441
  64.9 0.6 copy.14
  65.5 0.6 copy.15
  66.2 0.9 %copy.16 = f32[512,400]{0,1:T(8,128)} copy(f32[512,400]{0,1:T(8,128)S(1)} %bitcast.6) | data formatting | bytes 1638400
